TPU v7x, 512 devices: a whole 4x8x8 slice. The times are simulated.
512 devices in a mesh: wide: 64 (over z, y_lo, core), narrow: 8 (over y_hi, x).
Axes of the slice: x: 4, y: 8 (y_hi: 2, y_lo: 4; y = y_hi * 4 + y_lo), z: 8, core: 2. Of those that a mesh axis runs over, the one named last changes fastest.
Arguments:
- volume: float32 [256, 128, 1024], P('wide', 'narrow'), may hold values from -12 to 12
Outputs:
- smoothed: float32 [256, 128, 1024], P('wide', 'narrow')
All inputs are finite; a program needn't handle non-finite values.
Results may differ from a plain program's by a relative error of at most 0.00019.
Values sent between devices are 32-bit elements; how exact they have to be, the bound alone decides.
No kernel may reach another device: no remote copies, remote signals or barrier semaphores. Data moves between devices by JAX's collectives and lax.ppermute only.
A program may use at most 64 MiB of HBM per device.

v0:
```python
import jax
import jax.numpy as jnp
from jax import lax
from jax.sharding import PartitionSpec as P

step_weight = 300.0
contrast_sq = 9.0


def with_halo(shard, sides, width):
    for axis, dim in sides:
        count, length = (lax.axis_size(axis), shard.shape[dim])
        up = [(i, (i + 1) % count) for i in range(count - 1)]
        down = [(j, i) for i, j in up]
        last = lax.slice_in_dim(shard, length - width, length, axis=dim)
        first = lax.slice_in_dim(shard, 0, width, axis=dim)
        before = lax.ppermute(last, axis, up)
        after = lax.ppermute(first, axis, down)
        shard = jnp.concatenate([before, shard, after], axis=dim)
    return shard


def cyclic_solve(lower, diag, upper, values):
    length = values.shape[0]
    if length == 1:
        return values / diag
    middle = length // 2

    def halves(field):
        paired = field.reshape((middle, 2) + field.shape[1:])
        return (paired[:, 0], paired[:, 1])

    def after(field, filler):
        return jnp.concatenate([field[1:], jnp.full_like(field[:1], filler)], 0)

    lower_even, lower_odd = halves(lower)
    diag_even, diag_odd = halves(diag)
    upper_even, upper_odd = halves(upper)
    value_even, value_odd = halves(values)
    factor_left = -lower_odd / diag_even
    factor_right = -upper_odd / after(diag_even, 1.0)
    odd_part = cyclic_solve(
        factor_left * lower_even,
        diag_odd + factor_left * upper_even + factor_right * after(lower_even, 0.0),
        factor_right * after(upper_even, 0.0),
        value_odd + factor_left * value_even + factor_right * after(value_even, 0.0),
    )
    previous = jnp.concatenate([jnp.zeros_like(odd_part[:1]), odd_part[:-1]], 0)
    even_part = (value_even - lower_even * previous - upper_even * odd_part) / diag_even
    return jnp.stack([even_part, odd_part], 1).reshape(values.shape)


def diffuse(values, cond):
    between = 0.5 * (cond[:-1] + cond[1:])
    edge = jnp.zeros_like(cond[:1])
    lower = jnp.concatenate([edge, -step_weight * between], 0)
    upper = jnp.concatenate([-step_weight * between, edge], 0)
    return cyclic_solve(lower, 1.0 - lower - upper, upper, values)


def per_device(volume):
    inl, crs, tms = volume.shape
    wide_count = lax.axis_size("wide")
    narrow_count = lax.axis_size("narrow")
    wide_rank = lax.axis_index("wide")
    narrow_rank = lax.axis_index("narrow")
    padded = with_halo(volume, (("wide", 0), ("narrow", 1)), 1)
    first_row = jnp.where(wide_rank == 0, padded[1:2], padded[0:1])
    final_row = jnp.where(wide_rank == wide_count - 1, padded[-2:-1], padded[-1:])
    padded = jnp.concatenate([first_row, padded[1:-1], final_row], 0)
    first_col = jnp.where(narrow_rank == 0, padded[:, 1:2], padded[:, 0:1])
    final_col = jnp.where(narrow_rank == narrow_count - 1, padded[:, -2:-1], padded[:, -1:])
    padded = jnp.concatenate([first_col, padded[:, 1:-1], final_col], 1)
    power = (0.5 * (padded[2:, 1:-1] - padded[:-2, 1:-1])) ** 2
    power = power + (0.5 * (padded[1:-1, 2:] - padded[1:-1, :-2])) ** 2
    timed = jnp.concatenate([volume[:, :, :1], volume, volume[:, :, -1:]], 2)
    power = power + (0.5 * (timed[:, :, 2:] - timed[:, :, :-2])) ** 2
    cond = 1.0 / (1.0 + power / contrast_sq)
    traces = inl * crs
    solved = diffuse(volume.reshape(traces, tms).T, cond.reshape(traces, tms).T)
    along_time = solved.T.reshape(inl, crs, tms)
    columns = crs * tms
    lines = (
        lax.all_to_all(
            volume.reshape(inl, columns), "wide", split_axis=1, concat_axis=0, tiled=True
        ),
        lax.all_to_all(cond.reshape(inl, columns), "wide", split_axis=1, concat_axis=0, tiled=True),
    )
    solved = diffuse(lines[0], lines[1])
    along_inline = lax.all_to_all(solved, "wide", split_axis=0, concat_axis=1, tiled=True).reshape(
        inl, crs, tms
    )
    lines = (
        lax.all_to_all(volume, "narrow", split_axis=2, concat_axis=1, tiled=True),
        lax.all_to_all(cond, "narrow", split_axis=2, concat_axis=1, tiled=True),
    )
    solved = diffuse(jnp.transpose(lines[0], (1, 0, 2)), jnp.transpose(lines[1], (1, 0, 2)))
    along_cross = lax.all_to_all(
        jnp.transpose(solved, (1, 0, 2)), "narrow", split_axis=1, concat_axis=2, tiled=True
    )
    lateral = along_inline + along_cross
    return (lateral + along_time) / 3.0


def solution(mesh):
    placed = (P("wide", "narrow", None),)
    return jax.shard_map(
        per_device, mesh=mesh, in_specs=placed, out_specs=P("wide", "narrow", None), check_vma=False
    )
```

profile of v0, /device:TPU:1, one launch (start us, length us, event | category | flops | bytes accessed | tf_op | source)
XLA Modules:
  0.0 156.7 jit_solution(9909950086737457264)
XLA Ops:
  0.0 0.9 fusion.175
  0.9 4.6 %collective-permute-start = (f32[1,16,1024]{2,1,0:T(8,128)S(1)}, f32[1,16,1024]{2,1,0:T(8,128)S(1)}, u32[]{:S(2)}, u32[]{:S(2)}) collective-permute-start(f32[1,16,1024]{2,1,0:T(8,128)S(1)} %get-tuple-element.81), channel_id=1, source_target_pairs={{0,8},{8,16},{16,24},{24,32},{32,40},{40,48},{48,56},{56,64},{64,7... | collective-permute-start | bytes 196616 | tf_op jit(solution)/shard_map/ppermute | solution.py:17
  5.5 5.6 %collective-permute-start.1 = (f32[1,16,1024]{2,1,0:T(8,128)S(1)}, f32[1,16,1024]{2,1,0:T(8,128)S(1)}, u32[]{:S(2)}, u32[]{:S(2)}) collective-permute-start(f32[1,16,1024]{2,1,0:T(8,128)S(1)} %get-tuple-element.80), channel_id=1, source_target_pairs={{8,0},{16,8},{24,16},{32,24},{40,32},{48,40},{56,48},{64,56},{72,6... | collective-permute-start | bytes 196616 | tf_op jit(solution)/shard_map/ppermute | solution.py:18
  11.1 1.7 %copy.1462 = f32[4,16,1024]{1,0,2:T(4,128)S(1)} copy(f32[4,16,1024]{2,1,0:T(8,128)} %param.1) | data formatting | bytes 524288 | tf_op args[0]
  12.8 2.3 %reshape.948 = f32[8,1,8192]{2,1,0:T(1,128)} reshape(f32[1024,4,16]{2,1,0:T(4,128)S(1)} %bitcast.1584) | data formatting | bytes 524288
  15.1 4.8 %all-to-all-start.3 = ((f32[8,1,8192]{2,1,0:T(1,128)}), f32[8,1,8192]{2,1,0:T(1,128)S(1)}, u32[]{:S(2)}, u32[]{:S(2)}) async-start(f32[8,1,8192]{2,1,0:T(1,128)} %reshape.948), calls=%async_computation.3 | async-start | bytes 524288 | tf_op jit(solution)/shard_map/all_to_all | solution.py:94
  20.1 1.1 fusion.156
  21.4 3.4 %collective-permute-start.2 = (f32[6,1,1024]{2,1,0:T(1,128)S(1)}, f32[6,1,1024]{2,1,0:T(1,128)S(1)}, u32[]{:S(2)}, u32[]{:S(2)}) collective-permute-start(f32[6,1,1024]{2,1,0:T(1,128)S(1)} %get-tuple-element.38), channel_id=1, source_target_pairs={{0,1},{1,2},{2,3},{3,4},{4,5},{5,6},{6,7},{8,9},{9,10},{10,11},{11... | collective-permute-start | bytes 73736 | tf_op jit(solution)/shard_map/ppermute | solution.py:17
  24.7 1.3 collective-permute-start.3
  26.4 0.9 copy.1373
  27.3 2.4 %collective-permute-done.3 = f32[6,1,1024]{2,1,0:T(1,128)S(1)} collective-permute-done((f32[6,1,1024]{2,1,0:T(1,128)S(1)}, f32[6,1,1024]{2,1,0:T(1,128)S(1)}, u32[]{:S(2)}, u32[]{:S(2)}) %collective-permute-start.3) | collective-permute-done | bytes 24608 | tf_op jit(solution)/shard_map/ppermute | solution.py:18
  30.9 1.1 fusion.157
  38.5 18.1 %all-to-all-start = ((f32[4,64,256]{2,0,1:T(4,128)}), f32[4,64,256]{2,0,1:T(4,128)}, u32[]{:S(2)}, u32[]{:S(2)}) async-start(f32[4,64,256]{2,0,1:T(4,128)} %copy.1373), calls=%async_computation | async-start | bytes 524288 | tf_op jit(solution)/shard_map/all_to_all | solution.py:84
  58.0 2.3 %reshape.946 = f32[8,1,8192]{2,1,0:T(1,128)} reshape(f32[1024,4,16]{2,1,0:T(4,128)S(1)} %bitcast.1585) | data formatting | bytes 524288
  62.0 8.0 %all-to-all-done = f32[4,64,256]{2,0,1:T(4,128)} async-done(((f32[4,64,256]{2,0,1:T(4,128)}), f32[4,64,256]{2,0,1:T(4,128)}, u32[]{:S(2)}, u32[]{:S(2)}) %all-to-all-start) | async-done | bytes 262176 | tf_op jit(solution)/shard_map/all_to_all | solution.py:84
  70.0 13.6 %all-to-all-start.4 = ((f32[8,1,8192]{2,1,0:T(1,128)}), f32[8,1,8192]{2,1,0:T(1,128)}, u32[]{:S(2)}, u32[]{:S(2)}) async-start(f32[8,1,8192]{2,1,0:T(1,128)} %reshape.946), calls=%async_computation.4 | async-start | bytes 524288 | tf_op jit(solution)/shard_map/all_to_all | solution.py:95
  83.6 1.0 subtract_divide_fusion.2
  84.6 0.9 copy.1375
  87.0 1.3 reduce.1
  88.3 1.5 reshape.949
  91.3 0.9 fusion.163
  92.2 1.2 reshape.840
  94.2 7.3 %all-to-all-start.1 = ((f32[4,64,256]{2,0,1:T(4,128)}), f32[4,64,256]{2,0,1:T(4,128)}, u32[]{:S(2)}, u32[]{:S(2)}) async-start(f32[4,64,256]{2,0,1:T(4,128)} %copy.1375), calls=%async_computation.1 | async-start | bytes 524288 | tf_op jit(solution)/shard_map/all_to_all | solution.py:87
  101.5 2.3 %reduce = f32[8,8192]{1,0:T(8,128)S(1)} reduce(f32[8,1,8192]{2,1,0:T(1,128)} %all-to-all-done.4, f32[]{:T(128)} %broadcast.298), dimensions={1}, to_apply=%all_to_all.91.reduce_sub_computation | reduce | bytes 524292 | tf_op jit(solution)/shard_map/all_to_all | solution.py:95
  103.7 1.5 reshape.947
  110.7 4.2 %all-to-all-done.1 = f32[4,64,256]{2,0,1:T(4,128)} async-done(((f32[4,64,256]{2,0,1:T(4,128)}), f32[4,64,256]{2,0,1:T(4,128)}, u32[]{:S(2)}, u32[]{:S(2)}) %all-to-all-start.1) | async-done | bytes 262176 | tf_op jit(solution)/shard_map/all_to_all | solution.py:87
  114.9 7.8 %all-to-all-start.5 = ((f32[4,128,128]{2,0,1:T(4,128)}), f32[4,128,128]{2,0,1:T(4,128)S(1)}, u32[]{:S(2)}, u32[]{:S(2)}) async-start(f32[4,128,128]{2,0,1:T(4,128)} %copy.1542), calls=%async_computation.5 | async-start | bytes 524288 | tf_op jit(solution)/shard_map/all_to_all | solution.py:98
  122.7 1.0 all_to_all.83
  130.0 0.9 all_to_all.84
  130.9 1.8 %all-to-all-done.5 = f32[4,128,128]{2,0,1:T(4,128)S(1)} async-done(((f32[4,128,128]{2,0,1:T(4,128)}), f32[4,128,128]{2,0,1:T(4,128)S(1)}, u32[]{:S(2)}, u32[]{:S(2)}) %all-to-all-start.5) | async-done | bytes 262176 | tf_op jit(solution)/shard_map/all_to_all | solution.py:98
  132.8 9.6 %all-to-all-start.2 = ((f32[64,4,256]{2,1,0:T(4,128)}), f32[64,4,256]{2,1,0:T(4,128)S(1)}, u32[]{:S(2)}, u32[]{:S(2)}) async-start(f32[64,4,256]{2,1,0:T(4,128)} %all_to_all.84), calls=%async_computation.2 | async-start | bytes 524288 | tf_op jit(solution)/shard_map/all_to_all | solution.py:90
  143.6 12.3 %all-to-all-done.2 = f32[64,4,256]{2,1,0:T(4,128)S(1)} async-done(((f32[64,4,256]{2,1,0:T(4,128)}), f32[64,4,256]{2,1,0:T(4,128)S(1)}, u32[]{:S(2)}, u32[]{:S(2)}) %all-to-all-start.2) | async-done | bytes 262176 | tf_op jit(solution)/shard_map/all_to_all | solution.py:90
  (474 shorter events, 26.0 us)
Async XLA Ops:
  0.9 20.4 %collective-permute-start = (f32[1,16,1024]{2,1,0:T(8,128)S(1)}, f32[1,16,1024]{2,1,0:T(8,128)S(1)}, u32[]{:S(2)}, u32[]{:S(2)}) collective-permute-start(f32[1,16,1024]{2,1,0:T(8,128)S(1)} %get-tuple-element.81), channel_id=1, source_target_pairs={{0,8},{8,16},{16,24},{24,32},{32,40},{40,48},{48,56},{56,64},{64,7... | collective-permute-start | bytes 196616 | tf_op jit(solution)/shard_map/ppermute | solution.py:17
  5.5 14.4 %copy-start = (f32[4,16,1024]{2,1,0:T(8,128)S(1)}, f32[4,16,1024]{2,1,0:T(8,128)}, u32[]{:S(2)}) copy-start(f32[4,16,1024]{2,1,0:T(8,128)} %param.1) | copy-start | bytes 786436
  5.5 15.8 %collective-permute-start.1 = (f32[1,16,1024]{2,1,0:T(8,128)S(1)}, f32[1,16,1024]{2,1,0:T(8,128)S(1)}, u32[]{:S(2)}, u32[]{:S(2)}) collective-permute-start(f32[1,16,1024]{2,1,0:T(8,128)S(1)} %get-tuple-element.80), channel_id=1, source_target_pairs={{8,0},{16,8},{24,16},{32,24},{40,32},{48,40},{56,48},{64,56},{72,6... | collective-permute-start | bytes 196616 | tf_op jit(solution)/shard_map/ppermute | solution.py:18
  15.1 23.3 %all-to-all-start.3 = ((f32[8,1,8192]{2,1,0:T(1,128)}), f32[8,1,8192]{2,1,0:T(1,128)S(1)}, u32[]{:S(2)}, u32[]{:S(2)}) async-start(f32[8,1,8192]{2,1,0:T(1,128)} %reshape.948), calls=%async_computation.3 | async-start | bytes 524288 | tf_op jit(solution)/shard_map/all_to_all | solution.py:94
  21.4 5.9 %collective-permute-start.2 = (f32[6,1,1024]{2,1,0:T(1,128)S(1)}, f32[6,1,1024]{2,1,0:T(1,128)S(1)}, u32[]{:S(2)}, u32[]{:S(2)}) collective-permute-start(f32[6,1,1024]{2,1,0:T(1,128)S(1)} %get-tuple-element.38), channel_id=1, source_target_pairs={{0,1},{1,2},{2,3},{3,4},{4,5},{5,6},{6,7},{8,9},{9,10},{10,11},{11... | collective-permute-start | bytes 73736 | tf_op jit(solution)/shard_map/ppermute | solution.py:17
  24.7 4.9 %collective-permute-start.3 = (f32[6,1,1024]{2,1,0:T(1,128)S(1)}, f32[6,1,1024]{2,1,0:T(1,128)S(1)}, u32[]{:S(2)}, u32[]{:S(2)}) collective-permute-start(f32[6,1,1024]{2,1,0:T(1,128)S(1)} %get-tuple-element.39), channel_id=1, source_target_pairs={{1,0},{2,1},{3,2},{4,3},{5,4},{6,5},{7,6},{9,8},{10,9},{11,10},{12... | collective-permute-start | bytes 73736 | tf_op jit(solution)/shard_map/ppermute | solution.py:18
  33.0 1.0 copy-start.12
  34.4 1.2 copy-start.4
  35.8 1.2 copy-start.16
  36.0 1.1 copy-start.13
  36.4 1.1 copy-start.18
  36.6 1.8 %copy-start.23 = (f32[64,1,64]{2,1,0:T(1,128)}, f32[64,1,64]{2,1,0:T(1,128)S(1)}, u32[]{:S(2)}) copy-start(f32[64,1,64]{2,1,0:T(1,128)S(1)} %get-tuple-element.144) | copy-start | bytes 49156
  36.7 1.7 %copy-start.20 = (f32[64,1,64]{2,1,0:T(1,128)}, f32[64,1,64]{2,1,0:T(1,128)S(1)}, u32[]{:S(2)}) copy-start(f32[64,1,64]{2,1,0:T(1,128)S(1)} %get-tuple-element.146) | copy-start | bytes 49156
  36.8 19.7 %copy-start.24 = (f32[64,1,64]{2,1,0:T(1,128)}, f32[64,1,64]{2,1,0:T(1,128)S(1)}, u32[]{:S(2)}) copy-start(f32[64,1,64]{2,1,0:T(1,128)S(1)} %get-tuple-element.141) | copy-start | bytes 49156
  37.0 19.6 %copy-start.25 = (f32[64,1,64]{2,1,0:T(1,128)}, f32[64,1,64]{2,1,0:T(1,128)S(1)}, u32[]{:S(2)}) copy-start(f32[64,1,64]{2,1,0:T(1,128)S(1)} %get-tuple-element.148) | copy-start | bytes 49156
  38.4 18.1 %copy-start.14 = (f32[8,1,8192]{2,1,0:T(1,128)}, f32[8,1,8192]{2,1,0:T(1,128)S(1)}, u32[]{:S(2)}) copy-start(f32[8,1,8192]{2,1,0:T(1,128)S(1)} %all-to-all-done.3) | copy-start | bytes 786436
  38.5 31.5 %all-to-all-start = ((f32[4,64,256]{2,0,1:T(4,128)}), f32[4,64,256]{2,0,1:T(4,128)}, u32[]{:S(2)}, u32[]{:S(2)}) async-start(f32[4,64,256]{2,0,1:T(4,128)} %copy.1373), calls=%async_computation | async-start | bytes 524288 | tf_op jit(solution)/shard_map/all_to_all | solution.py:84
  60.3 26.7 %copy-start.15 = (f32[8,1,8192]{2,1,0:T(1,128)S(1)}, f32[8,1,8192]{2,1,0:T(1,128)}, u32[]{:S(2)}) copy-start(f32[8,1,8192]{2,1,0:T(1,128)} %copy-done.14) | copy-start | bytes 786436
  70.0 24.2 %all-to-all-start.4 = ((f32[8,1,8192]{2,1,0:T(1,128)}), f32[8,1,8192]{2,1,0:T(1,128)}, u32[]{:S(2)}, u32[]{:S(2)}) async-start(f32[8,1,8192]{2,1,0:T(1,128)} %reshape.946), calls=%async_computation.4 | async-start | bytes 524288 | tf_op jit(solution)/shard_map/all_to_all | solution.py:95
  93.4 8.1 %copy-start.2 = (f32[128,2,256]{2,1,0:T(2,128)}, f32[128,2,256]{2,1,0:T(2,128)S(1)}, u32[]{:S(2)}) copy-start(f32[128,2,256]{2,1,0:T(2,128)S(1)} %reshape.840) | copy-start | bytes 786436
  94.2 20.7 %all-to-all-start.1 = ((f32[4,64,256]{2,0,1:T(4,128)}), f32[4,64,256]{2,0,1:T(4,128)}, u32[]{:S(2)}, u32[]{:S(2)}) async-start(f32[4,64,256]{2,0,1:T(4,128)} %copy.1375), calls=%async_computation.1 | async-start | bytes 524288 | tf_op jit(solution)/shard_map/all_to_all | solution.py:87
  106.0 1.1 copy-start.22
  106.0 1.2 copy-start.8
  106.1 1.2 copy-start.19
  109.8 14.3 %copy-start.3 = (f32[128,2,256]{2,1,0:T(2,128)S(1)}, f32[128,2,256]{2,1,0:T(2,128)}, u32[]{:S(2)}) copy-start(f32[128,2,256]{2,1,0:T(2,128)} %copy-done.2) | copy-start | bytes 786436
  114.9 17.9 %all-to-all-start.5 = ((f32[4,128,128]{2,0,1:T(4,128)}), f32[4,128,128]{2,0,1:T(4,128)S(1)}, u32[]{:S(2)}, u32[]{:S(2)}) async-start(f32[4,128,128]{2,0,1:T(4,128)} %copy.1542), calls=%async_computation.5 | async-start | bytes 524288 | tf_op jit(solution)/shard_map/all_to_all | solution.py:98
  124.1 1.4 copy-start.21
  129.3 13.0 %copy-start.1 = (f32[128,2,64]{2,1,0:T(2,128)S(1)}, f32[128,2,64]{2,1,0:T(2,128)}, u32[]{:S(2)}) copy-start(f32[128,2,64]{2,1,0:T(2,128)} %copy.1654) | copy-start | bytes 196612
  129.3 13.0 %copy-start.5 = (f32[256,1,64]{2,1,0:T(1,128)S(1)}, f32[256,1,64]{2,1,0:T(1,128)}, u32[]{:S(2)}) copy-start(f32[256,1,64]{2,1,0:T(1,128)} %copy-done.4) | copy-start | bytes 196612
  129.3 13.0 %copy-start.7 = (f32[256,1,64]{2,1,0:T(1,128)S(1)}, f32[256,1,64]{2,1,0:T(1,128)}, u32[]{:S(2)}) copy-start(f32[256,1,64]{2,1,0:T(1,128)} %copy-done.6) | copy-start | bytes 196612
  129.3 13.0 %copy-start.10 = (f32[256,1,64]{2,1,0:T(1,128)S(1)}, f32[256,1,64]{2,1,0:T(1,128)}, u32[]{:S(2)}) copy-start(f32[256,1,64]{2,1,0:T(1,128)} %copy-done.9) | copy-start | bytes 196612
  132.8 23.1 %all-to-all-start.2 = ((f32[64,4,256]{2,1,0:T(4,128)}), f32[64,4,256]{2,1,0:T(4,128)S(1)}, u32[]{:S(2)}, u32[]{:S(2)}) async-start(f32[64,4,256]{2,1,0:T(4,128)} %all_to_all.84), calls=%async_computation.2 | async-start | bytes 524288 | tf_op jit(solution)/shard_map/all_to_all | solution.py:90
  (4 other events, 3.4 us)
where the time goes:
time: 158 us; the launch traced here: 157 us
  starting transfers between devices  76 us (48%)
  local copies, waits for them, and re-layouts  37.5 us (24%)
  waiting for transfers between devices  28.7 us (18%)
  other arithmetic  11.2 us (7%)
  between operations  3.48 us (2%)
    all_to_all x1, starting transfers between devices, per_device(): lax.all_to_all(volume.reshape(inl, columns), 'wide', split_axis=1, concat...  18.1 us
    all_to_all x1, starting transfers between devices, per_device(): lax.all_to_all(cond, 'narrow', split_axis=2, concat_axis=1, tiled=True)  13.6 us
    all_to_all x1, waiting for transfers between devices, per_device(): lax.all_to_all(solved, 'wide', split_axis=0, concat_axis=1, tiled=True)  12.3 us
    unnamed x116, local copies, waits for them, and re-layouts  10.2 us
    all_to_all x1, starting transfers between devices, per_device(): lax.all_to_all(solved, 'wide', split_axis=0, concat_axis=1, tiled=True)  9.56 us
    slice x69, local copies, waits for them, and re-layouts, halves(): return (paired[:, 0], paired[:, 1])  8.12 us
    all_to_all x1, waiting for transfers between devices, per_device(): lax.all_to_all(volume.reshape(inl, columns), 'wide', split_axis=1, concat...  7.98 us
    ppermute x2, starting transfers between devices, with_halo(): before = lax.ppermute(last, axis, up)  7.96 us
  transfers between devices with their start and end apart: 10, of which 5 were waited for; matrix products, arithmetic and copies ran while one was open for 28% of the time, Pallas kernels for 0%

commit v1 on v0

--- a/solution.py
+++ b/solution.py
@@ -1,10 +1,28 @@
+import functools
 import jax
 import jax.numpy as jnp
 from jax import lax
 from jax.sharding import PartitionSpec as P
+from jax.lax import all_to_all, axis_size
 
 step_weight = 300.0
 contrast_sq = 9.0
+
+
+def mix_zone(inp, array_axis, in_dim):
+    aux = jnp.concatenate(
+        all_to_all(
+            jnp.stack(jnp.split(inp, axis_size("wide"), axis=array_axis)),
+            concat_axis=0,
+            axis_name="wide",
+            split_axis=0,
+        ),
+        axis=in_dim,
+    )
+    return aux
+
+
+_enter_yards = functools.partial(mix_zone, array_axis=1, in_dim=0)
 
 
 def with_halo(shard, sides, width):
@@ -81,9 +99,7 @@
     along_time = solved.T.reshape(inl, crs, tms)
     columns = crs * tms
     lines = (
-        lax.all_to_all(
-            volume.reshape(inl, columns), "wide", split_axis=1, concat_axis=0, tiled=True
-        ),
+        _enter_yards(volume.reshape(inl, columns)),
         lax.all_to_all(cond.reshape(inl, columns), "wide", split_axis=1, concat_axis=0, tiled=True),
     )
     solved = diffuse(lines[0], lines[1])

time: 158 us -> 199 us (1.26)
  local copies, waits for them, and re-layouts: 37.5 us -> 80.6 us
    unnamed x116 -> x182, local copies, waits for them, and re-layouts: 10.2 us -> 48.4 us
    all_to_all x1, waiting for transfers between devices: 7.98 us -> 0.01 us  [mix_zone(): all_to_all(jnp.stack(jnp.split(inp, axis_size('wide'), axis=array_axis)),...]
    all_to_all x1, starting transfers between devices: 7.28 us -> 14 us  [per_device(): lax.all_to_all(cond.reshape(inl, columns), 'wide', split_axis=1, concat_a...]
    all_to_all x1, waiting for transfers between devices: 0.01 us -> 6.33 us  [per_device(): lax.all_to_all(cond, 'narrow', split_axis=2, concat_axis=1, tiled=True)]
    all_to_all x1, starting transfers between devices: 7.79 us -> 3.41 us  [per_device(): lax.all_to_all(jnp.transpose(solved, (1, 0, 2)), 'narrow', split_axis=1,...]
    slice x69 -> x70, local copies, waits for them, and re-layouts: 8.12 us -> 8.77 us  [halves(): return (paired[:, 0], paired[:, 1])]
  transfers between devices with their start and end apart: 10 -> 10, of which waited for: 5 -> 5; matrix products, arithmetic and copies ran while one was open for 28% -> 43% of each run, Pallas kernels for 0% -> 0%
where the time goes in v1:
time: 199 us; the launch traced here: 198 us
  local copies, waits for them, and re-layouts  80.6 us (41%)
  starting transfers between devices  77.6 us (39%)
  waiting for transfers between devices  26.8 us (13%)
  other arithmetic  9.26 us (5%)
  between operations  3.48 us (2%)
    unnamed x182, local copies, waits for them, and re-layouts  48.4 us
    all_to_all x1, starting transfers between devices, mix_zone(): all_to_all(jnp.stack(jnp.split(inp, axis_size('wide'), axis=array_axis)),...  18.3 us
    all_to_all x1, starting transfers between devices, per_device(): lax.all_to_all(cond.reshape(inl, columns), 'wide', split_axis=1, concat_a...  14 us
    all_to_all x1, starting transfers between devices, per_device(): lax.all_to_all(cond, 'narrow', split_axis=2, concat_axis=1, tiled=True)  13.6 us
    all_to_all x1, waiting for transfers between devices, per_device(): lax.all_to_all(solved, 'wide', split_axis=0, concat_axis=1, tiled=True)  12.3 us
    slice x70, local copies, waits for them, and re-layouts, halves(): return (paired[:, 0], paired[:, 1])  8.77 us
    all_to_all x1, starting transfers between devices, per_device(): lax.all_to_all(solved, 'wide', split_axis=0, concat_axis=1, tiled=True)  8.49 us
    ppermute x2, starting transfers between devices, with_halo(): before = lax.ppermute(last, axis, up)  7.95 us
  transfers between devices with their start and end apart: 10, of which 5 were waited for; matrix products, arithmetic and copies ran while one was open for 43% of the time, Pallas kernels for 0%

profile of v1, /device:TPU:1, one launch (start us, length us, event | category | flops | bytes accessed | tf_op | source)
XLA Modules:
  0.0 197.7 jit_solution(7811611022381900841)
XLA Ops:
  0.0 1.5 fusion.175
  1.5 4.6 %collective-permute-start = (f32[1,16,1024]{2,1,0:T(8,128)S(1)}, f32[1,16,1024]{2,1,0:T(8,128)}, u32[]{:S(2)}, u32[]{:S(2)}) collective-permute-start(f32[1,16,1024]{2,1,0:T(8,128)S(1)} %get-tuple-element.81), channel_id=1, source_target_pairs={{0,8},{8,16},{16,24},{24,32},{32,40},{40,48},{48,56},{56,64},{64,7... | collective-permute-start | bytes 196616 | tf_op jit(solution)/shard_map/ppermute | solution.py:35
  6.1 6.2 %collective-permute-start.1 = (f32[1,16,1024]{2,1,0:T(8,128)}, f32[1,16,1024]{2,1,0:T(8,128)}, u32[]{:S(2)}, u32[]{:S(2)}) collective-permute-start(f32[1,16,1024]{2,1,0:T(8,128)} %get-tuple-element.80), channel_id=1, source_target_pairs={{8,0},{16,8},{24,16},{32,24},{40,32},{48,40},{56,48},{64,56},{72,6... | collective-permute-start | bytes 196616 | tf_op jit(solution)/shard_map/ppermute | solution.py:36
  12.3 1.7 copy.1454
  14.0 2.3 %reshape.942 = f32[8,1,8192]{2,1,0:T(1,128)} reshape(f32[1024,4,16]{2,1,0:T(4,128)S(1)} %bitcast.1843) | data formatting | bytes 524288
  16.3 4.4 %all-to-all-start.3 = ((f32[8,1,8192]{2,1,0:T(1,128)}), f32[8,1,8192]{2,1,0:T(1,128)S(1)}, u32[]{:S(2)}, u32[]{:S(2)}) async-start(f32[8,1,8192]{2,1,0:T(1,128)} %reshape.942), calls=%async_computation.3 | async-start | bytes 524288 | tf_op jit(solution)/shard_map/all_to_all | solution.py:110
  57.8 1.1 fusion.156
  61.2 3.4 %collective-permute-start.2 = (f32[6,1,1024]{2,1,0:T(1,128)S(1)}, f32[6,1,1024]{2,1,0:T(1,128)S(1)}, u32[]{:S(2)}, u32[]{:S(2)}) collective-permute-start(f32[6,1,1024]{2,1,0:T(1,128)S(1)} %get-tuple-element.38), channel_id=1, source_target_pairs={{0,1},{1,2},{2,3},{3,4},{4,5},{5,6},{6,7},{8,9},{9,10},{10,11},{11... | collective-permute-start | bytes 73736 | tf_op jit(solution)/shard_map/ppermute | solution.py:35
  64.6 1.3 collective-permute-start.3
  66.7 2.5 %collective-permute-done.3 = f32[6,1,1024]{2,1,0:T(1,128)S(1)} collective-permute-done((f32[6,1,1024]{2,1,0:T(1,128)S(1)}, f32[6,1,1024]{2,1,0:T(1,128)S(1)}, u32[]{:S(2)}, u32[]{:S(2)}) %collective-permute-start.3) | collective-permute-done | bytes 24608 | tf_op jit(solution)/shard_map/ppermute | solution.py:36
  70.4 1.1 fusion.157
  78.0 18.3 %all-to-all-start = ((f32[64,4,256]{2,1,0:T(4,128)}), f32[64,4,256]{2,1,0:T(4,128)}, u32[]{:S(2)}, u32[]{:S(2)}) async-start(f32[64,4,256]{2,1,0:T(4,128)} %constant_dynamic-update-slice_fusion), calls=%async_computation | async-start | bytes 524288 | tf_op jit(solution)/shard_map/all_to_all | solution.py:14
  98.6 2.3 %reshape.940 = f32[8,1,8192]{2,1,0:T(1,128)} reshape(f32[1024,4,16]{2,1,0:T(4,128)S(1)} %bitcast.1840) | data formatting | bytes 524288
  100.8 1.8 copy.1367
  105.1 2.1 %reduce.1 = f32[8,8192]{1,0:T(8,128)S(1)} reduce(f32[8,1,8192]{2,1,0:T(1,128)} %copy-done.14, f32[]{:T(128)} %broadcast.298), dimensions={1}, to_apply=%all_to_all.76.reduce_sub_computation | reduce | bytes 524292 | tf_op jit(solution)/shard_map/all_to_all | solution.py:110
  107.2 1.5 reshape.943
  110.2 13.6 %all-to-all-start.4 = ((f32[8,1,8192]{2,1,0:T(1,128)}), f32[8,1,8192]{2,1,0:T(1,128)S(1)}, u32[]{:S(2)}, u32[]{:S(2)}) async-start(f32[8,1,8192]{2,1,0:T(1,128)} %reshape.940), calls=%async_computation.4 | async-start | bytes 524288 | tf_op jit(solution)/shard_map/all_to_all | solution.py:111
  123.8 0.9 fusion.163
  124.7 1.2 reshape_reshape.3
  126.6 0.9 fusion.166
  127.5 6.3 %all-to-all-done.4 = f32[8,1,8192]{2,1,0:T(1,128)S(1)} async-done(((f32[8,1,8192]{2,1,0:T(1,128)}), f32[8,1,8192]{2,1,0:T(1,128)S(1)}, u32[]{:S(2)}, u32[]{:S(2)}) %all-to-all-start.4) | async-done | bytes 262176 | tf_op jit(solution)/shard_map/all_to_all | solution.py:111
  133.8 14.0 %all-to-all-start.1 = ((f32[4,64,256]{2,0,1:T(4,128)}), f32[4,64,256]{2,0,1:T(4,128)}, u32[]{:S(2)}, u32[]{:S(2)}) async-start(f32[4,64,256]{2,0,1:T(4,128)} %copy.1367), calls=%async_computation.1 | async-start | bytes 524288 | tf_op jit(solution)/shard_map/all_to_all | solution.py:103
  147.8 1.2 reduce
  149.0 1.5 reshape.941
  155.1 0.9 copy.1534
  156.0 5.3 %all-to-all-done.1 = f32[4,64,256]{2,0,1:T(4,128)} async-done(((f32[4,64,256]{2,0,1:T(4,128)}), f32[4,64,256]{2,0,1:T(4,128)}, u32[]{:S(2)}, u32[]{:S(2)}) %all-to-all-start.1) | async-done | bytes 262176 | tf_op jit(solution)/shard_map/all_to_all | solution.py:103
  161.3 3.4 %all-to-all-start.5 = ((f32[4,128,128]{2,0,1:T(4,128)}), f32[4,128,128]{2,0,1:T(4,128)S(1)}, u32[]{:S(2)}, u32[]{:S(2)}) async-start(f32[4,128,128]{2,0,1:T(4,128)} %copy.1534), calls=%async_computation.5 | async-start | bytes 524288 | tf_op jit(solution)/shard_map/all_to_all | solution.py:114
  164.7 1.0 all_to_all.72
  168.0 0.9 copy_bitcast_fusion.10
  173.4 0.9 all_to_all.73
  174.8 8.5 %all-to-all-start.2 = ((f32[64,4,256]{2,1,0:T(4,128)}), f32[64,4,256]{2,1,0:T(4,128)S(1)}, u32[]{:S(2)}, u32[]{:S(2)}) async-start(f32[64,4,256]{2,1,0:T(4,128)} %all_to_all.73), calls=%async_computation.2 | async-start | bytes 524288 | tf_op jit(solution)/shard_map/all_to_all | solution.py:106
  184.6 12.3 %all-to-all-done.2 = f32[64,4,256]{2,1,0:T(4,128)S(1)} async-done(((f32[64,4,256]{2,1,0:T(4,128)}), f32[64,4,256]{2,1,0:T(4,128)S(1)}, u32[]{:S(2)}, u32[]{:S(2)}) %all-to-all-start.2) | async-done | bytes 262176 | tf_op jit(solution)/shard_map/all_to_all | solution.py:106
  (540 shorter events, 65.5 us)
Async XLA Ops:
  1.5 58.0 %collective-permute-start = (f32[1,16,1024]{2,1,0:T(8,128)S(1)}, f32[1,16,1024]{2,1,0:T(8,128)}, u32[]{:S(2)}, u32[]{:S(2)}) collective-permute-start(f32[1,16,1024]{2,1,0:T(8,128)S(1)} %get-tuple-element.81), channel_id=1, source_target_pairs={{0,8},{8,16},{16,24},{24,32},{32,40},{40,48},{48,56},{56,64},{64,7... | collective-permute-start | bytes 196616 | tf_op jit(solution)/shard_map/ppermute | solution.py:35
  6.1 14.6 %copy-start = (f32[4,16,1024]{2,1,0:T(8,128)S(1)}, f32[4,16,1024]{2,1,0:T(8,128)}, u32[]{:S(2)}) copy-start(f32[4,16,1024]{2,1,0:T(8,128)} %param.1) | copy-start | bytes 786436
  6.1 54.2 %collective-permute-start.1 = (f32[1,16,1024]{2,1,0:T(8,128)}, f32[1,16,1024]{2,1,0:T(8,128)}, u32[]{:S(2)}, u32[]{:S(2)}) collective-permute-start(f32[1,16,1024]{2,1,0:T(8,128)} %get-tuple-element.80), channel_id=1, source_target_pairs={{8,0},{16,8},{24,16},{32,24},{40,32},{48,40},{56,48},{64,56},{72,6... | collective-permute-start | bytes 196616 | tf_op jit(solution)/shard_map/ppermute | solution.py:36
  16.3 61.7 %all-to-all-start.3 = ((f32[8,1,8192]{2,1,0:T(1,128)}), f32[8,1,8192]{2,1,0:T(1,128)S(1)}, u32[]{:S(2)}, u32[]{:S(2)}) async-start(f32[8,1,8192]{2,1,0:T(1,128)} %reshape.942), calls=%async_computation.3 | async-start | bytes 524288 | tf_op jit(solution)/shard_map/all_to_all | solution.py:110
  61.2 5.5 %collective-permute-start.2 = (f32[6,1,1024]{2,1,0:T(1,128)S(1)}, f32[6,1,1024]{2,1,0:T(1,128)S(1)}, u32[]{:S(2)}, u32[]{:S(2)}) collective-permute-start(f32[6,1,1024]{2,1,0:T(1,128)S(1)} %get-tuple-element.38), channel_id=1, source_target_pairs={{0,1},{1,2},{2,3},{3,4},{4,5},{5,6},{6,7},{8,9},{9,10},{10,11},{11... | collective-permute-start | bytes 73736 | tf_op jit(solution)/shard_map/ppermute | solution.py:35
  64.6 4.6 %collective-permute-start.3 = (f32[6,1,1024]{2,1,0:T(1,128)S(1)}, f32[6,1,1024]{2,1,0:T(1,128)S(1)}, u32[]{:S(2)}, u32[]{:S(2)}) collective-permute-start(f32[6,1,1024]{2,1,0:T(1,128)S(1)} %get-tuple-element.39), channel_id=1, source_target_pairs={{1,0},{2,1},{3,2},{4,3},{5,4},{6,5},{7,6},{9,8},{10,9},{11,10},{12... | collective-permute-start | bytes 73736 | tf_op jit(solution)/shard_map/ppermute | solution.py:36
  72.5 1.0 copy-start.11
  73.9 1.2 copy-start.2
  75.4 1.1 copy-start.15
  75.5 1.0 copy-start.12
  78.0 18.3 %copy-start.22 = (f32[32,2,64]{2,1,0:T(2,128)}, f32[32,2,64]{2,1,0:T(2,128)S(1)}, u32[]{:S(2)}) copy-start(f32[32,2,64]{2,1,0:T(2,128)S(1)} %copy.1640) | copy-start | bytes 49156
  78.0 18.3 %copy-start.14 = (f32[8,1,8192]{2,1,0:T(1,128)}, f32[8,1,8192]{2,1,0:T(1,128)S(1)}, u32[]{:S(2)}) copy-start(f32[8,1,8192]{2,1,0:T(1,128)S(1)} %all-to-all-done.3) | copy-start | bytes 786436
  78.0 32.2 %all-to-all-start = ((f32[64,4,256]{2,1,0:T(4,128)}), f32[64,4,256]{2,1,0:T(4,128)}, u32[]{:S(2)}, u32[]{:S(2)}) async-start(f32[64,4,256]{2,1,0:T(4,128)} %constant_dynamic-update-slice_fusion), calls=%async_computation | async-start | bytes 524288 | tf_op jit(solution)/shard_map/all_to_all | solution.py:14
  98.6 4.1 %copy-start.23 = (f32[32,2,64]{2,1,0:T(2,128)S(1)}, f32[32,2,64]{2,1,0:T(2,128)}, u32[]{:S(2)}) copy-start(f32[32,2,64]{2,1,0:T(2,128)} %copy-done.22) | copy-start | bytes 49156
  98.6 4.1 %copy-start.26 = (f32[64,1,64]{2,0,1:T(8,128)S(1)}, f32[64,1,64]{2,0,1:T(8,128)}, u32[]{:S(2)}) copy-start(f32[64,1,64]{2,0,1:T(8,128)} %divide_bitcast_fusion.2) | copy-start | bytes 49156
  98.6 4.2 %copy-start.13 = (f32[128,1,64]{2,1,0:T(1,128)S(1)}, f32[128,1,64]{2,1,0:T(1,128)}, u32[]{:S(2)}) copy-start(f32[128,1,64]{2,1,0:T(1,128)} %copy-done.12) | copy-start | bytes 98308
  98.6 4.2 %copy-start.16 = (f32[128,1,64]{2,1,0:T(1,128)S(1)}, f32[128,1,64]{2,1,0:T(1,128)}, u32[]{:S(2)}) copy-start(f32[128,1,64]{2,1,0:T(1,128)} %copy-done.15) | copy-start | bytes 98308
  98.6 4.2 %copy-start.18 = (f32[128,1,64]{2,1,0:T(1,128)S(1)}, f32[128,1,64]{2,1,0:T(1,128)}, u32[]{:S(2)}) copy-start(f32[128,1,64]{2,1,0:T(1,128)} %copy-done.17) | copy-start | bytes 98308
  110.2 23.6 %all-to-all-start.4 = ((f32[8,1,8192]{2,1,0:T(1,128)}), f32[8,1,8192]{2,1,0:T(1,128)S(1)}, u32[]{:S(2)}, u32[]{:S(2)}) async-start(f32[8,1,8192]{2,1,0:T(1,128)} %reshape.940), calls=%async_computation.4 | async-start | bytes 524288 | tf_op jit(solution)/shard_map/all_to_all | solution.py:111
  133.8 27.5 %all-to-all-start.1 = ((f32[4,64,256]{2,0,1:T(4,128)}), f32[4,64,256]{2,0,1:T(4,128)}, u32[]{:S(2)}, u32[]{:S(2)}) async-start(f32[4,64,256]{2,0,1:T(4,128)} %copy.1367), calls=%async_computation.1 | async-start | bytes 524288 | tf_op jit(solution)/shard_map/all_to_all | solution.py:103
  151.3 1.1 copy-start.25
  151.3 1.2 copy-start.7
  151.4 1.2 copy-start.21
  161.3 13.5 %all-to-all-start.5 = ((f32[4,128,128]{2,0,1:T(4,128)}), f32[4,128,128]{2,0,1:T(4,128)S(1)}, u32[]{:S(2)}, u32[]{:S(2)}) async-start(f32[4,128,128]{2,0,1:T(4,128)} %copy.1534), calls=%async_computation.5 | async-start | bytes 524288 | tf_op jit(solution)/shard_map/all_to_all | solution.py:114
  165.9 2.1 %copy-start.24 = (f32[127,1,256]{2,1,0:T(1,128)S(1)}, f32[127,1,256]{2,1,0:T(1,128)}, u32[]{:S(2)}) copy-start(f32[127,1,256]{2,1,0:T(1,128)} %slice.1816) | copy-start | bytes 390148
  166.1 2.8 %copy-start.6 = (f32[128,1,256]{2,1,0:T(1,128)S(1)}, f32[128,1,256]{2,1,0:T(1,128)}, u32[]{:S(2)}) copy-start(f32[128,1,256]{2,1,0:T(1,128)} %get-tuple-element.58) | copy-start | bytes 393220
  166.1 2.8 %copy-start.20 = (f32[128,1,256]{2,1,0:T(1,128)S(1)}, f32[128,1,256]{2,1,0:T(1,128)}, u32[]{:S(2)}) copy-start(f32[128,1,256]{2,1,0:T(1,128)} %get-tuple-element.59) | copy-start | bytes 393220
  172.7 10.6 %copy-start.1 = (f32[128,2,64]{2,1,0:T(2,128)S(1)}, f32[128,2,64]{2,1,0:T(2,128)}, u32[]{:S(2)}) copy-start(f32[128,2,64]{2,1,0:T(2,128)} %copy.1646) | copy-start | bytes 196612
  172.7 10.6 %copy-start.3 = (f32[256,1,64]{2,1,0:T(1,128)S(1)}, f32[256,1,64]{2,1,0:T(1,128)}, u32[]{:S(2)}) copy-start(f32[256,1,64]{2,1,0:T(1,128)} %copy-done.2) | copy-start | bytes 196612
  172.7 10.6 %copy-start.5 = (f32[256,1,64]{2,1,0:T(1,128)S(1)}, f32[256,1,64]{2,1,0:T(1,128)}, u32[]{:S(2)}) copy-start(f32[256,1,64]{2,1,0:T(1,128)} %copy-done.4) | copy-start | bytes 196612
  172.8 10.6 %copy-start.9 = (f32[256,1,64]{2,1,0:T(1,128)S(1)}, f32[256,1,64]{2,1,0:T(1,128)}, u32[]{:S(2)}) copy-start(f32[256,1,64]{2,1,0:T(1,128)} %copy-done.8) | copy-start | bytes 196612
  174.8 22.0 %all-to-all-start.2 = ((f32[64,4,256]{2,1,0:T(4,128)}), f32[64,4,256]{2,1,0:T(4,128)S(1)}, u32[]{:S(2)}, u32[]{:S(2)}) async-start(f32[64,4,256]{2,1,0:T(4,128)} %all_to_all.73), calls=%async_computation.2 | async-start | bytes 524288 | tf_op jit(solution)/shard_map/all_to_all | solution.py:106
  (5 other events, 4.4 us)
